TPU v7x, 32 devices: a whole 2x2x4 slice. The times are simulated.
32 devices in a mesh: groups: 2 (over y), dp: 16 (over z, x, core).
Axes of the slice: x: 2, y: 2, z: 4, core: 2. Of those that a mesh axis runs over, the one named last changes fastest.
Arguments:
- layer_inputs: bfloat16 [1024, 14336], P(('groups', 'dp')), parts along dimension 0, may hold values from -6 to 6
- output_gradient_rows: bfloat16 [1024, 4096], P(('groups', 'dp')), parts along dimension 0, may hold values from -6 to 6
- eig_in: bfloat16 [14336, 14336], P(None, 'dp'), may hold values from -0.046875 to 0.046875
- eig_out: bfloat16 [4096, 4096], P('dp'), may hold values from -0.09375 to 0.09375
- lengths: int32 [8], P('groups'), parts along dimension 0, may hold values from 1 to 128, 384 in all
Outputs:
- corrections: float32 [28672, 4096], P(('groups', 'dp')), parts along dimension 0
There are 2 independent parts, one for each index of `groups`. A program takes and returns all parts, laid end to end along the dimension named above; an argument that names none is the same for every part. Nothing has to cross between parts.
Inputs may be any that keep to these rules, and one draw needn't show every extreme that they name: `lengths`: each sequence has 128 token slots; slots at or past its length are padding, and some sequence is full.
All inputs are finite; a program needn't handle non-finite values.
Results may differ from a plain program's by a relative error of at most 0.0038.
Values may be sent and summed in bfloat16 or wider, within the bound.
A program may use at most 128 MiB of HBM per device.

v0:
```python
import jax
import jax.numpy as jnp
from jax import lax
from jax.sharding import PartitionSpec as P

SEQ_LEN = 128
NSEQ = 4


def on_device(layer_inputs, output_gradient_rows, eig_in, eig_out, lengths):
    input_projection = jnp.dot(
        lax.all_gather(layer_inputs, "dp", axis=0, tiled=True),
        eig_in,
        preferred_element_type=jnp.float32,
    ).astype(jnp.bfloat16)
    slot_index = jnp.arange(SEQ_LEN, dtype=jnp.int32)
    live_mask = slot_index[None, :] < lengths[:, None]
    input_projection = input_projection.reshape(NSEQ, SEQ_LEN, input_projection.shape[1])
    input_projection = jnp.where(
        live_mask[:, :, None], input_projection, jnp.zeros_like(input_projection)
    )
    out_basis = lax.all_to_all(eig_out, "dp", split_axis=1, concat_axis=0, tiled=True)
    own_columns = jnp.dot(
        lax.all_gather(output_gradient_rows, "dp", axis=0, tiled=True),
        out_basis,
        preferred_element_type=jnp.float32,
    ).astype(jnp.bfloat16)
    projected = lax.all_gather(own_columns, "dp", axis=1, tiled=True)
    right_side_rows = projected.reshape(NSEQ, SEQ_LEN, projected.shape[1])
    sequence_gradient = jnp.einsum(
        "fer,feq->frq", input_projection, right_side_rows, preferred_element_type=jnp.float32
    )
    return jnp.sum(sequence_gradient * sequence_gradient, axis=0) / (NSEQ * SEQ_LEN)


def solution(mesh):
    placed = (
        P(("groups", "dp"), None),
        P(("groups", "dp"), None),
        P(None, "dp"),
        P("dp", None),
        P("groups"),
    )
    return jax.shard_map(
        on_device, mesh=mesh, in_specs=placed, out_specs=P(("groups", "dp"), None), check_vma=False
    )
```

profile of v0, /device:TPU:0, one launch (start us, length us, event | category | flops | bytes accessed | tf_op | source)
XLA Modules:
  0.0 293.7 jit_solution(5643981253814746006)
XLA Ops:
  6.5 0.0 copy-start
  6.5 0.0 all-gather.6.cloned.1.call-start
  6.5 0.7 all-gather.6.cloned.1.call-update
  7.3 0.0 all-gather.4.cloned.1.call-start
  7.3 0.7 all-gather.4.cloned.1.call-update
  8.0 0.0 all-gather.8.cloned.1.call-start
  8.1 4.1 %copy.9 = bf16[256,4096]{0,1:T(8,128)(2,1)} copy(bf16[256,4096]{1,0:T(8,128)(2,1)} %param.8) | data formatting | bytes 4194304 | tf_op args[3]
  12.1 80.0 %all_to_all.19 = bf16[256,16,256]{0,2,1:T(8,128)(2,1)S(1)} all-to-all(bf16[256,16,256]{0,2,1:T(8,128)(2,1)} %bitcast.11), channel_id=1, replica_groups=mesh['groups'=2,'dp'=16] {'dp'}, dimensions={1} | all-to-all | bytes 4194304 | tf_op jit(solution)/shard_map/all_to_all | solution.py:22
  92.1 2.4 copy.10
  94.5 0.0 all-gather.6.cloned.1.call-done
  94.5 5.0 %convolution_convert_fusion.1 = bf16[512,256]{1,0:T(8,128)(2,1)} fusion(bf16[512,4096]{1,0:T(8,128)(2,1)} %all-gather.6.cloned.1.call-done, bf16[4096,256]{1,0:T(8,128)(2,1)} %bitcast.12), kind=kOutput, calls=%fused_computation.3 | convolution fusion | flops 1073872896 | bytes 6553600 | tf_op jit(solution)/shard_map/dot_general | solution.py:23
  99.5 0.0 all-gather.8.cloned.1.call-update
  99.5 0.0 copy-done
  99.5 0.1 iota_compare_fusion
  99.6 103.9 %all-gather.4.cloned.1.call-done = bf16[512,14336]{1,0:T(8,128)(2,1)} async-done(((bf16[32,14336]{1,0:T(8,128)(2,1)}), bf16[512,14336]{1,0:T(8,128)(2,1)}) %all-gather.4.cloned.1.call-update) | async-done | bytes 14680080 | tf_op jit(solution)/shard_map/all_gather | solution.py:12
  203.5 21.0 %convolution_convert_fusion = bf16[512,896]{1,0:T(8,128)(2,1)S(1)} fusion(bf16[512,14336]{1,0:T(8,128)(2,1)} %all-gather.4.cloned.1.call-done, bf16[14336,896]{1,0:T(8,128)(2,1)} %param.7), kind=kOutput, calls=%fused_computation.2 | convolution fusion | flops 13153796096 | bytes 41287680 | tf_op jit(solution)/shard_map/dot_general | solution.py:11
  224.6 0.6 copy.8
  225.2 31.9 %all-gather.8.cloned.1.call-done = bf16[512,4096]{1,0:T(8,128)(2,1)} async-done(((bf16[512,256]{1,0:T(8,128)(2,1)}), bf16[512,4096]{1,0:T(8,128)(2,1)}) %all-gather.8.cloned.1.call-update) | async-done | bytes 4194320 | tf_op jit(solution)/shard_map/all_gather | solution.py:28
  257.1 16.6 %multiply_reduce_fusion = f32[896,4096]{1,0:T(8,128)} fusion(bf16[4,128,4096]{2,1,0:T(8,128)(2,1)} %bitcast.14, bf16[4,128,896]{1,2,0:T(8,128)(2,1)S(1)} %copy.8, pred[4,128]{1,0:T(4,128)(4,1)S(1)} %iota_compare_fusion), kind=kOutput, calls=%fused_computation | convolution fusion | flops 3784245248 | bytes 19792384 | tf_op jit(solution)/shard_map/fer,feq->frq/dot_general | solution.py:30
  273.8 13.4 %broadcast_multiply_fusion = f32[896,4096]{1,0:T(8,128)} fusion(f32[896,4096]{1,0:T(8,128)} %multiply_reduce_fusion), kind=kLoop, calls=%fused_computation.1 | loop fusion | flops 3670016 | bytes 29360128 | tf_op jit(solution)/shard_map/div | solution.py:33
Async XLA Ops:
  6.5 93.0 %copy-start = (s32[4]{0:T(128)S(1)}, s32[4]{0:T(128)}, u32[]{:S(2)}) copy-start(s32[4]{0:T(128)} %param.9) | copy-start | bytes 52
  6.5 87.9 %all-gather.6.cloned.1.call-start = ((), (), s32[]{:S(2)}) async-start(), calls=%async_computation.2 | async-start | bytes 4456448 | tf_op jit(solution)/shard_map/all_gather | solution.py:24
  7.3 196.3 %all-gather.4.cloned.1.call-start = ((), (), s32[]{:S(2)}) async-start(), calls=%async_computation.1 | async-start | bytes 15597568 | tf_op jit(solution)/shard_map/all_gather | solution.py:12
  8.0 249.1 %all-gather.8.cloned.1.call-start = ((), (), s32[]{:S(2)}) async-start(), calls=%async_computation.3 | async-start | bytes 4456448 | tf_op jit(solution)/shard_map/all_gather | solution.py:28
Sparse Core Ops, SparseCore 0:
  9.5 78.9 all-gather.5
  90.8 112.6 all-gather.3
  205.7 51.3 all-gather.7
where the time goes:
time: 294 us
  waiting for transfers between devices  137 us (47%)
  blocking collectives  80 us (27%)
  matrix products  42.6 us (14%)
  other arithmetic  13.5 us (5%)
  between operations  13.1 us (4%)
  local copies, waits for them, and re-layouts  7.07 us (2%)
    all_gather x1, waiting for transfers between devices, on_device(): lax.all_gather(layer_inputs, 'dp', axis=0, tiled=True)  104 us
    all_to_all x1, blocking collectives, on_device(): lax.all_to_all(eig_out, 'dp', split_axis=1, concat_axis=0, tiled=True)  80 us
    all_gather x1, waiting for transfers between devices, on_device(): projected = lax.all_gather(own_columns, 'dp', axis=1, tiled=True)  31.9 us
    dot_general x1, matrix products, on_device(): jnp.dot(lax.all_gather(layer_inputs, 'dp', axis=0, tiled=True), eig_in, p...  21 us
    dot_general x1, matrix products, on_device(): jnp.einsum('fer,feq->frq', input_projection, right_side_rows, preferred_e...  16.6 us
    div x1, other arithmetic, on_device(): jnp.sum(sequence_gradient * sequence_gradient, axis=0) / (NSEQ * SEQ_LEN)  13.4 us
  transfers between devices with their start and end apart: 3, of which 2 were waited for; matrix products, arithmetic and copies ran while one was open for 11% of the time, Pallas kernels for 0%

commit v1 on v0

--- a/solution.py
+++ b/solution.py
@@ -1,10 +1,318 @@
+import functools
+
 import jax
 import jax.numpy as jnp
 from jax import lax
+from jax.experimental import pallas as pl
+from jax.experimental.pallas import tpu as pltpu
 from jax.sharding import PartitionSpec as P
 
 SEQ_LEN = 128
 NSEQ = 4
+LANES = 2
+GROUPS = 4
+MESH = pl.DeviceIdType.MESH
+
+
+def gather_kernel(
+    n, x_ref, g_ref, ein_ref, eout_ref, pin_ref, pout_ref,
+    xb, gb, pb, eoc, einv, acc,
+    barrier_free, loc_sem, ein_sem, eo_send, eo_recv, eo_fwd,
+    xs_ring, xr_ring, xs_sib, xr_sib,
+    gs_ring, gr_ring, gs_sib, gr_sib,
+    ps_ring, pr_ring, ps_sib, pr_sib,
+):
+    del barrier_free
+    chips = n // 2
+    side = chips // 2
+    grp = lax.axis_index("groups")
+    me = lax.axis_index("dp")
+    core = lax.rem(me, 2)
+    chip = me // 2
+    cx = lax.rem(chip, 2)
+    cz = chip // 2
+    pos = cz * (1 - cx) + (chips - 1 - cz) * cx
+
+    def device_at(position, which_core):
+        q = lax.rem(position + 2 * chips, chips)
+        qx = q // side
+        qz = q * (1 - qx) + (chips - 1 - q) * qx
+        return (qz * 2 + qx) * 2 + which_core
+
+    nxt = (device_at(pos + 1, core), device_at(pos - 1, core))
+    sib = chip * 2 + (1 - core)
+
+    rows, din = x_ref.shape
+    half = rows // 2
+    kc = din // (LANES * GROUPS)
+    local = []
+    for h in range(2):
+        local.append(pltpu.make_async_copy(
+            g_ref.at[pl.ds(h * half, half)], gb.at[me, h], loc_sem.at[h]))
+    for j in range(LANES * GROUPS):
+        for h in range(2):
+            local.append(pltpu.make_async_copy(
+                x_ref.at[pl.ds(h * half, half), pl.ds(j * kc, kc)], xb.at[j, me, h],
+                loc_sem.at[2 + j * 2 + h]))
+    eh = eout_ref.shape[0] // 2
+    ec = eout_ref.shape[1] // n
+    nl = 2 + 2 * LANES * GROUPS
+    my_rows = pl.ds(pl.multiple_of(grp * eh, 16), eh)
+    local.append(pltpu.make_async_copy(
+        eout_ref.at[my_rows, pl.ds(pl.multiple_of(me * ec, 128), ec)], eoc.at[me, grp],
+        loc_sem.at[nl]))
+    for c in local:
+        c.start()
+    ein_copies = [
+        pltpu.make_async_copy(ein_ref.at[pl.ds(j * kc, kc)], einv.at[j], ein_sem.at[j])
+        for j in range(LANES * GROUPS)
+    ]
+    for c in ein_copies:
+        c.start()
+
+    barrier = pltpu.get_barrier_semaphore()
+    for k in range(1, n):
+        pl.semaphore_signal(barrier, inc=1, device_id=(grp, lax.rem(me + k, n)), device_id_type=MESH)
+    pl.semaphore_signal(barrier, inc=1, device_id=(1 - grp, me), device_id_type=MESH)
+    pl.semaphore_wait(barrier, n)
+
+    for c in local:
+        c.wait()
+
+    def eo_copy(k):
+        to = lax.rem(me + k, n)
+        return pltpu.make_async_remote_copy(
+            src_ref=eout_ref.at[my_rows, pl.ds(pl.multiple_of(to * ec, 128), ec)],
+            dst_ref=eoc.at[me, grp],
+            send_sem=eo_send.at[k], recv_sem=eo_recv.at[k],
+            device_id=(grp, to), device_id_type=MESH)
+
+    def ring_copy(item, d, s):
+        buf, sends, recvs, _, _ = item
+        src = device_at(pos - s if d == 0 else pos + s, core)
+        block = buf.at[src, d]
+        return pltpu.make_async_remote_copy(
+            src_ref=block, dst_ref=block,
+            send_sem=sends.at[d, s], recv_sem=recvs.at[d, s],
+            device_id=(grp, nxt[d]), device_id_type=MESH)
+
+    def sib_copy(item, d, s):
+        buf, _, _, sends, recvs = item
+        src = device_at(pos - s if d == 0 else pos + s, core)
+        block = buf.at[src, d]
+        return pltpu.make_async_remote_copy(
+            src_ref=block, dst_ref=block,
+            send_sem=sends.at[d, s], recv_sem=recvs.at[d, s],
+            device_id=(grp, sib), device_id_type=MESH)
+
+    def wait_ring(item, d, s):
+        buf, sends, recvs, _, _ = item
+        src = device_at(pos - s - 1 if d == 0 else pos + s + 1, core)
+        block = buf.at[src, d]
+        pltpu.make_async_remote_copy(
+            src_ref=block, dst_ref=block, send_sem=sends.at[d, s], recv_sem=recvs.at[d, s],
+            device_id=(grp, nxt[d]), device_id_type=MESH).wait_recv()
+
+    def wait_sib(item, d, s):
+        buf, _, _, sends, recvs = item
+        src = device_at(pos - s if d == 0 else pos + s, 1 - core)
+        block = buf.at[src, d]
+        pltpu.make_async_remote_copy(
+            src_ref=block, dst_ref=block, send_sem=sends.at[d, s], recv_sem=recvs.at[d, s],
+            device_id=(grp, sib), device_id_type=MESH).wait_recv()
+
+    def stage(items, piece=None):
+        for item in items:
+            for d in range(2):
+                ring_copy(item, d, 0).start()
+        for item in items:
+            for d in range(2):
+                sib_copy(item, d, 0).start()
+
+        def hop(s, carry):
+            if piece is not None:
+                piece(s - 1)
+            for item in items:
+                for d in range(2):
+                    wait_ring(item, d, s - 1)
+
+                    @pl.when(s < chips - 1)
+                    def _():
+                        ring_copy(item, d, s).start()
+
+                    sib_copy(item, d, s).start()
+            return carry
+
+        lax.fori_loop(1, chips, hop, 0)
+        if piece is not None:
+            piece(chips - 1)
+
+        def finish(s, carry):
+            for item in items:
+                for d in range(2):
+                    wait_sib(item, d, s)
+                    sib_copy(item, d, s).wait_send()
+
+                    @pl.when(s < chips - 1)
+                    def _():
+                        ring_copy(item, d, s).wait_send()
+            return carry
+
+        lax.fori_loop(0, chips, finish, 0)
+
+    def x_items(g):
+        return [
+            (xb.at[g * LANES + w], xs_ring.at[w], xr_ring.at[g, w], xs_sib.at[w], xr_sib.at[g, w])
+            for w in range(LANES)
+        ]
+
+    tiles = chips // LANES
+    per = n // tiles
+    mt = per * rows
+
+    def multiply(g, p):
+        j = g * LANES + p // tiles
+        m = lax.rem(p, tiles)
+        lhs = xb[j, pl.ds(m * per, per)].reshape(mt, kc)
+        at = pl.ds(pl.multiple_of(m * mt, mt), mt)
+        acc[at, :] += jnp.dot(lhs, einv[j], preferred_element_type=jnp.float32)
+
+    g_item = (gb, gs_ring, gr_ring, gs_sib, gr_sib)
+    p_item = (pb, ps_ring, pr_ring, ps_sib, pr_sib)
+
+    for k in range(1, n):
+        eo_copy(k).start()
+    stage([g_item] + x_items(0))
+
+    for k in range(1, n):
+        eo_copy(k).wait()
+    fwd = pltpu.make_async_remote_copy(
+        src_ref=eoc.at[:, grp], dst_ref=eoc.at[:, grp],
+        send_sem=eo_fwd.at[0], recv_sem=eo_fwd.at[1],
+        device_id=(1 - grp, me), device_id_type=MESH)
+    fwd.start()
+    acc[...] = jnp.zeros_like(acc)
+    for c in ein_copies:
+        c.wait()
+    fwd.wait()
+
+    def own(m, carry):
+        lhs = gb[pl.ds(m * (n // 4), n // 4)].reshape(rows * n // 4, gb.shape[3])
+        rhs = eoc[...].reshape(n * 2 * eh, ec)
+        res = jnp.dot(lhs, rhs, preferred_element_type=jnp.float32).astype(jnp.bfloat16)
+        at = pl.ds(pl.multiple_of(lax.rem(m, 2) * (rows * n // 4), 16), rows * n // 4)
+        pb[me, m // 2, at, :] = res
+        return carry
+
+    lax.fori_loop(0, 4, own, 0)
+    stage([p_item] + x_items(1), functools.partial(multiply, 0))
+    out_copy = pltpu.make_async_copy(pb, pout_ref, loc_sem.at[0])
+    out_copy.start()
+
+    def group(g, carry):
+        stage(x_items(g), functools.partial(multiply, g - 1))
+        return carry
+
+    lax.fori_loop(2, GROUPS, group, 0)
+
+    def tail(p, carry):
+        multiply(GROUPS - 1, p)
+        return carry
+
+    lax.fori_loop(0, chips, tail, 0)
+    pin_ref[...] = acc[...].astype(jnp.bfloat16)
+    out_copy.wait()
+
+
+def project(n, x, g, ein, eout):
+    rows, din = x.shape
+    dout = g.shape[1]
+    tokens = rows * n
+    cols = ein.shape[1]
+    chips = n // 2
+    ec = dout // n
+    nchunk = LANES * GROUPS
+    kc = din // nchunk
+    dma = pltpu.SemaphoreType.DMA
+    ring = (2, chips - 1)
+    sib = (2, chips)
+    return pl.pallas_call(
+        functools.partial(gather_kernel, n),
+        out_shape=(
+            jax.ShapeDtypeStruct((tokens, cols), jnp.bfloat16),
+            jax.ShapeDtypeStruct((n, 2, tokens // 2, ec), jnp.bfloat16),
+        ),
+        in_specs=[pl.BlockSpec(memory_space=pl.ANY)] * 4,
+        out_specs=(
+            pl.BlockSpec(memory_space=pltpu.VMEM),
+            pl.BlockSpec(memory_space=pl.ANY),
+        ),
+        scratch_shapes=[
+            pltpu.VMEM((nchunk, n, 2, rows // 2, kc), jnp.bfloat16),
+            pltpu.VMEM((n, 2, rows // 2, dout), jnp.bfloat16),
+            pltpu.VMEM((n, 2, tokens // 2, ec), jnp.bfloat16),
+            pltpu.VMEM((n, 2, eout.shape[0] // 2, ec), jnp.bfloat16),
+            pltpu.VMEM((nchunk, kc, cols), jnp.bfloat16),
+            pltpu.VMEM((tokens, cols), jnp.float32),
+            pltpu.SemaphoreType.REGULAR,
+            dma((3 + 2 * nchunk,)),
+            dma((nchunk,)),
+            dma((n,)),
+            dma((n,)),
+            dma((2,)),
+            dma((LANES,) + ring), dma((GROUPS, LANES) + ring),
+            dma((LANES,) + sib), dma((GROUPS, LANES) + sib),
+            dma(ring), dma(ring), dma(sib), dma(sib),
+            dma(ring), dma(ring), dma(sib), dma(sib),
+        ],
+        compiler_params=pltpu.CompilerParams(
+            collective_id=0, has_side_effects=True, vmem_limit_bytes=60 * 1024 * 1024
+        ),
+        cost_estimate=pl.CostEstimate(
+            flops=2 * tokens * (din * cols + dout * ec),
+            bytes_accessed=2 * din * cols, transcendentals=0),
+    )(x, g, ein, eout)
+
+
+def correction_kernel(seq_len, nseq, len_ref, pin_ref, p_ref, out_ref, left):
+    @pl.when(pl.program_id(0) == 0)
+    def _():
+        for s in range(nseq):
+            block = pin_ref[pl.ds(s * seq_len, seq_len), :].astype(jnp.float32)
+            slot = lax.broadcasted_iota(jnp.int32, block.shape, 0)
+            block = jnp.where(slot < len_ref[s], block, 0.0)
+            left[s] = block.T.astype(jnp.bfloat16)
+
+    total = None
+    for s in range(nseq):
+        grad = jnp.dot(
+            left[s], p_ref[0, pl.ds(s * seq_len, seq_len), :], preferred_element_type=jnp.float32
+        )
+        total = grad * grad if total is None else total + grad * grad
+    out_ref[...] = total * (1.0 / (nseq * seq_len))
+
+
+def correct(pin, p, lengths):
+    n, tokens, ec = p.shape
+    cols = pin.shape[1]
+    return pl.pallas_call(
+        functools.partial(correction_kernel, SEQ_LEN, NSEQ),
+        grid=(n,),
+        out_shape=jax.ShapeDtypeStruct((cols, n * ec), jnp.float32),
+        in_specs=[
+            pl.BlockSpec(memory_space=pltpu.SMEM),
+            pl.BlockSpec((tokens, cols), lambda i: (0, 0)),
+            pl.BlockSpec((1, tokens, ec), lambda i: (i, 0, 0)),
+        ],
+        out_specs=pl.BlockSpec((cols, ec), lambda i: (0, i)),
+        scratch_shapes=[pltpu.VMEM((NSEQ, cols, SEQ_LEN), jnp.bfloat16)],
+        compiler_params=pltpu.CompilerParams(vmem_limit_bytes=40 * 1024 * 1024),
+    )(lengths, pin, p)
+
+
+def on_device_kernels(n, x, g, ein, eout, lengths):
+    pin, p = project(n, x, g, ein, eout)
+    return correct(pin, p.reshape(n, p.shape[1] * p.shape[2], p.shape[3]), lengths)
 
 
 def on_device(layer_inputs, output_gradient_rows, eig_in, eig_out, lengths):
@@ -41,6 +349,11 @@
         P("dp", None),
         P("groups"),
     )
+    n = mesh.shape["dp"]
+    if mesh.shape["groups"] == 2 and n == 16:
+        body = functools.partial(on_device_kernels, n)
+    else:
+        body = on_device
     return jax.shard_map(
-        on_device, mesh=mesh, in_specs=placed, out_specs=P(("groups", "dp"), None), check_vma=False
+        body, mesh=mesh, in_specs=placed, out_specs=P(("groups", "dp"), None), check_vma=False
     )

time: 294 us -> 221 us (0.75)
  Pallas kernels: 0 us -> 217 us
  waiting for transfers between devices: 137 us -> 0 us
  blocking collectives: 80 us -> 0 us
  matrix products: 42.6 us -> 0 us
  other arithmetic: 13.5 us -> 0 us
  between operations: 13.1 us -> 0.03 us
  local copies, waits for them, and re-layouts: 7.07 us -> 3.36 us
    pallas_call x0 -> x2, Pallas kernels: none -> 217 us  [the longest x1 203 us: project(): pl.pallas_call(functools.partial(gather_kernel, n), out_shape=(jax.ShapeD...]
    all_gather x3 -> x0, waiting for transfers between devices: 136 us -> none  [the longest x1 104 us: on_device(): lax.all_gather(layer_inputs, 'dp', axis=0, tiled=True)]
    all_to_all x1 -> x0, blocking collectives: 80 us -> none  [on_device(): lax.all_to_all(eig_out, 'dp', split_axis=1, concat_axis=0, tiled=True)]
    dot_general x3 -> x0, matrix products: 42.6 us -> none  [the longest x1 21 us: on_device(): jnp.dot(lax.all_gather(layer_inputs, 'dp', axis=0, tiled=True), eig_in, p...]
    div x1 -> x0, other arithmetic: 13.4 us -> none  [on_device(): jnp.sum(sequence_gradient * sequence_gradient, axis=0) / (NSEQ * SEQ_LEN)]
  transfers between devices with their start and end apart: 3 -> 0, of which waited for: 2 -> 0; matrix products, arithmetic and copies ran while one was open for 11% -> 0% of each run, Pallas kernels for 0% -> 0%
where the time goes in v1:
time: 221 us; the launch traced here: 220 us
  Pallas kernels  217 us (98%)
  local copies, waits for them, and re-layouts  3.36 us (2%)
    pallas_call x1, Pallas kernels, project(): pl.pallas_call(functools.partial(gather_kernel, n), out_shape=(jax.ShapeD...  203 us
    pallas_call x1, Pallas kernels, correct(): pl.pallas_call(functools.partial(correction_kernel, SEQ_LEN, NSEQ), grid=...  14 us

profile of v1, /device:TPU:0, one launch (start us, length us, event | category | flops | bytes accessed | tf_op | source)
XLA Modules:
  0.0 220.4 jit_solution(17565868107383454014)
XLA Ops:
  0.0 0.0 copy-start.2
  0.0 203.0 %shard_map.55 = (bf16[512,896]{1,0:T(8,128)(2,1)}, bf16[16,2,256,256]{3,2,1,0:T(8,128)(2,1)}) custom-call(bf16[32,14336]{1,0:T(8,128)(2,1)} %x_ref.1, bf16[32,4096]{1,0:T(8,128)(2,1)} %g_ref.1, bf16[14336,896]{1,0:T(8,128)(2,1)} %ein_ref.1, bf16[256,4096]{1,0:T(8,128)(2,1)} %eout_ref.1), custom_call_target="tpu_custom_call" | custom-call | flops 14227079168 | bytes 25690112 | tf_op jit(solution)/shard_map/pallas_call | solution.py:239
  203.0 0.0 copy-done.2
  203.1 0.0 copy-start
  203.1 2.2 copy-done
  205.2 0.0 copy-start.1
  205.3 1.2 copy-done.1
  206.4 14.0 %shard_map.56 = f32[896,4096]{1,0:T(8,128)} custom-call(s32[4]{0:T(128)S(1)} %copy-done.2, bf16[512,896]{1,0:T(8,128)(2,1)S(1)} %copy-done.1, bf16[16,512,256]{2,1,0:T(8,128)(2,1)S(1)} %bitcast.1), custom_call_target="tpu_custom_call" | custom-call | tf_op jit(solution)/shard_map/pallas_call | solution.py:298
Async XLA Ops:
  0.0 203.1 %copy-start.2 = (s32[4]{0:T(128)S(1)}, s32[4]{0:T(128)}, u32[]{:S(2)}) copy-start(s32[4]{0:T(128)} %len_ref.1) | copy-start | bytes 52
  203.1 2.2 copy-start
  205.2 1.2 copy-start.1

commit v2 on v1

--- a/solution.py
+++ b/solution.py
@@ -9,15 +9,15 @@
 
 SEQ_LEN = 128
 NSEQ = 4
-LANES = 2
-GROUPS = 4
+LANES = 4
+GROUPS = 2
 MESH = pl.DeviceIdType.MESH
 
 
 def gather_kernel(
     n, x_ref, g_ref, ein_ref, eout_ref, pin_ref, pout_ref,
     xb, gb, pb, eoc, einv, acc,
-    barrier_free, loc_sem, ein_sem, eo_send, eo_recv, eo_fwd,
+    barrier_free, loc_sem, ein_sem, eo_send, eo_recv, fwd_send, fwd_recv,
     xs_ring, xr_ring, xs_sib, xr_sib,
     gs_ring, gr_ring, gs_sib, gr_sib,
     ps_ring, pr_ring, ps_sib, pr_sib,
@@ -121,7 +121,7 @@
             src_ref=block, dst_ref=block, send_sem=sends.at[d, s], recv_sem=recvs.at[d, s],
             device_id=(grp, sib), device_id_type=MESH).wait_recv()
 
-    def stage(items, piece=None):
+    def begin(items):
         for item in items:
             for d in range(2):
                 ring_copy(item, d, 0).start()
@@ -129,6 +129,7 @@
             for d in range(2):
                 sib_copy(item, d, 0).start()
 
+    def stage(items, piece=None, last=None):
         def hop(s, carry):
             if piece is not None:
                 piece(s - 1)
@@ -144,8 +145,8 @@
             return carry
 
         lax.fori_loop(1, chips, hop, 0)
-        if piece is not None:
-            piece(chips - 1)
+        if last is not None:
+            last(chips - 1)
 
         def finish(s, carry):
             for item in items:
@@ -174,27 +175,40 @@
         j = g * LANES + p // tiles
         m = lax.rem(p, tiles)
         lhs = xb[j, pl.ds(m * per, per)].reshape(mt, kc)
-        at = pl.ds(pl.multiple_of(m * mt, mt), mt)
+        at = pl.ds(pl.multiple_of(m * mt, 128), mt)
         acc[at, :] += jnp.dot(lhs, einv[j], preferred_element_type=jnp.float32)
 
     g_item = (gb, gs_ring, gr_ring, gs_sib, gr_sib)
     p_item = (pb, ps_ring, pr_ring, ps_sib, pr_sib)
 
+    def fwd_copy(k, part):
+        src = lax.rem(me - k + n, n)
+        return pltpu.make_async_remote_copy(
+            src_ref=eoc.at[src, part], dst_ref=eoc.at[src, part],
+            send_sem=fwd_send.at[k], recv_sem=fwd_recv.at[k],
+            device_id=(1 - grp, me), device_id_type=MESH)
+
+    def hand_on(s):
+        for k in (2 * s + 1, 2 * s + 2):
+            eo_copy(k).wait()
+            fwd_copy(k, grp).start()
+
+    fwd_copy(0, grp).start()
+    begin([g_item])
     for k in range(1, n):
         eo_copy(k).start()
-    stage([g_item] + x_items(0))
-
-    for k in range(1, n):
-        eo_copy(k).wait()
-    fwd = pltpu.make_async_remote_copy(
-        src_ref=eoc.at[:, grp], dst_ref=eoc.at[:, grp],
-        send_sem=eo_fwd.at[0], recv_sem=eo_fwd.at[1],
-        device_id=(1 - grp, me), device_id_type=MESH)
-    fwd.start()
+    begin(x_items(0))
+    stage([g_item] + x_items(0), hand_on)
+    eo_copy(n - 1).wait()
+    fwd_copy(n - 1, grp).start()
+
+    begin(x_items(1))
     acc[...] = jnp.zeros_like(acc)
     for c in ein_copies:
         c.wait()
-    fwd.wait()
+    for k in range(n):
+        fwd_copy(k, grp).wait_send()
+        fwd_copy(k, 1 - grp).wait_recv()
 
     def own(m, carry):
         lhs = gb[pl.ds(m * (n // 4), n // 4)].reshape(rows * n // 4, gb.shape[3])
@@ -205,15 +219,11 @@
         return carry
 
     lax.fori_loop(0, 4, own, 0)
-    stage([p_item] + x_items(1), functools.partial(multiply, 0))
+    begin([p_item])
+    piece = functools.partial(multiply, 0)
+    stage([p_item] + x_items(1), piece, piece)
     out_copy = pltpu.make_async_copy(pb, pout_ref, loc_sem.at[0])
     out_copy.start()
-
-    def group(g, carry):
-        stage(x_items(g), functools.partial(multiply, g - 1))
-        return carry
-
-    lax.fori_loop(2, GROUPS, group, 0)
 
     def tail(p, carry):
         multiply(GROUPS - 1, p)
@@ -259,7 +269,8 @@
             dma((nchunk,)),
             dma((n,)),
             dma((n,)),
-            dma((2,)),
+            dma((n,)),
+            dma((n,)),
             dma((LANES,) + ring), dma((GROUPS, LANES) + ring),
             dma((LANES,) + sib), dma((GROUPS, LANES) + sib),
             dma(ring), dma(ring), dma(sib), dma(sib),

time: 221 us -> 182 us (0.82)
  Pallas kernels: 217 us -> 178 us
    pallas_call x1, Pallas kernels: 203 us -> 164 us  [project(): pl.pallas_call(functools.partial(gather_kernel, n), out_shape=(jax.ShapeD...]
where the time goes in v2:
time: 182 us
  Pallas kernels  178 us (98%)
  local copies, waits for them, and re-layouts  3.36 us (2%)
    pallas_call x1, Pallas kernels, project(): pl.pallas_call(functools.partial(gather_kernel, n), out_shape=(jax.ShapeD...  164 us
    pallas_call x1, Pallas kernels, correct(): pl.pallas_call(functools.partial(correction_kernel, SEQ_LEN, NSEQ), grid=...  14 us

profile of v2, /device:TPU:0, one launch (start us, length us, event | category | flops | bytes accessed | tf_op | source)
XLA Modules:
  0.0 181.8 jit_solution(9764596654890993134)
XLA Ops:
  0.0 0.0 copy-start.2
  0.0 164.4 %shard_map.55 = (bf16[512,896]{1,0:T(8,128)(2,1)}, bf16[16,2,256,256]{3,2,1,0:T(8,128)(2,1)}) custom-call(bf16[32,14336]{1,0:T(8,128)(2,1)} %x_ref.1, bf16[32,4096]{1,0:T(8,128)(2,1)} %g_ref.1, bf16[14336,896]{1,0:T(8,128)(2,1)} %ein_ref.1, bf16[256,4096]{1,0:T(8,128)(2,1)} %eout_ref.1), custom_call_target="tpu_custom_call" | custom-call | flops 14227079168 | bytes 25690112 | tf_op jit(solution)/shard_map/pallas_call | solution.py:249
  164.5 0.0 copy-done.2
  164.5 0.0 copy-start
  164.5 2.2 %copy-done = bf16[16,2,256,256]{3,2,1,0:T(8,128)(2,1)S(1)} copy-done((bf16[16,2,256,256]{3,2,1,0:T(8,128)(2,1)S(1)}, bf16[16,2,256,256]{3,2,1,0:T(8,128)(2,1)}, u32[]{:S(2)}) %copy-start) | copy-done | bytes 4194328
  166.7 0.0 copy-start.1
  166.7 1.2 copy-done.1
  167.8 14.0 %shard_map.56 = f32[896,4096]{1,0:T(8,128)} custom-call(s32[4]{0:T(128)S(1)} %copy-done.2, bf16[512,896]{1,0:T(8,128)(2,1)S(1)} %copy-done.1, bf16[16,512,256]{2,1,0:T(8,128)(2,1)S(1)} %bitcast.1), custom_call_target="tpu_custom_call" | custom-call | tf_op jit(solution)/shard_map/pallas_call | solution.py:309
Async XLA Ops:
  0.0 164.5 %copy-start.2 = (s32[4]{0:T(128)S(1)}, s32[4]{0:T(128)}, u32[]{:S(2)}) copy-start(s32[4]{0:T(128)} %len_ref.1) | copy-start | bytes 52
  164.5 2.2 %copy-start = (bf16[16,2,256,256]{3,2,1,0:T(8,128)(2,1)S(1)}, bf16[16,2,256,256]{3,2,1,0:T(8,128)(2,1)}, u32[]{:S(2)}) copy-start(bf16[16,2,256,256]{3,2,1,0:T(8,128)(2,1)} %get-tuple-element.8) | copy-start | bytes 12582916
  166.7 1.2 copy-start.1

commit v3 on v2

--- a/solution.py
+++ b/solution.py
@@ -163,7 +163,7 @@
 
     def x_items(g):
         return [
-            (xb.at[g * LANES + w], xs_ring.at[w], xr_ring.at[g, w], xs_sib.at[w], xr_sib.at[g, w])
+            (xb.at[g * LANES + w], xs_ring.at[g, w], xr_ring.at[g, w], xs_sib.at[g, w], xr_sib.at[g, w])
             for w in range(LANES)
         ]
 
@@ -192,6 +192,10 @@
         for k in (2 * s + 1, 2 * s + 2):
             eo_copy(k).wait()
             fwd_copy(k, grp).start()
+
+        @pl.when(s == chips - 3)
+        def _():
+            begin(x_items(1))
 
     fwd_copy(0, grp).start()
     begin([g_item])
@@ -202,7 +206,6 @@
     eo_copy(n - 1).wait()
     fwd_copy(n - 1, grp).start()
 
-    begin(x_items(1))
     acc[...] = jnp.zeros_like(acc)
     for c in ein_copies:
         c.wait()
@@ -271,8 +274,8 @@
             dma((n,)),
             dma((n,)),
             dma((n,)),
-            dma((LANES,) + ring), dma((GROUPS, LANES) + ring),
-            dma((LANES,) + sib), dma((GROUPS, LANES) + sib),
+            dma((GROUPS, LANES) + ring), dma((GROUPS, LANES) + ring),
+            dma((GROUPS, LANES) + sib), dma((GROUPS, LANES) + sib),
             dma(ring), dma(ring), dma(sib), dma(sib),
             dma(ring), dma(ring), dma(sib), dma(sib),
         ],
@@ -317,7 +320,7 @@
         ],
         out_specs=pl.BlockSpec((cols, ec), lambda i: (0, i)),
         scratch_shapes=[pltpu.VMEM((NSEQ, cols, SEQ_LEN), jnp.bfloat16)],
-        compiler_params=pltpu.CompilerParams(vmem_limit_bytes=40 * 1024 * 1024),
+        compiler_params=pltpu.CompilerParams(vmem_limit_bytes=60 * 1024 * 1024),
     )(lengths, pin, p)
 
 

time: 182 us -> 188 us (1.033)
  Pallas kernels: 178 us -> 187 us
  local copies, waits for them, and re-layouts: 3.36 us -> 0 us
    pallas_call x1, Pallas kernels: 164 us -> 170 us  [project(): pl.pallas_call(functools.partial(gather_kernel, n), out_shape=(jax.ShapeD...]
    unnamed x6 -> x0, local copies, waits for them, and re-layouts: 3.36 us -> none
    pallas_call x1, Pallas kernels: 14 us -> 16.9 us  [correct(): pl.pallas_call(functools.partial(correction_kernel, SEQ_LEN, NSEQ), grid=...]
where the time goes in v3:
time: 188 us; the launch traced here: 187 us
  Pallas kernels  187 us (99%)
    pallas_call x1, Pallas kernels, project(): pl.pallas_call(functools.partial(gather_kernel, n), out_shape=(jax.ShapeD...  170 us
    pallas_call x1, Pallas kernels, correct(): pl.pallas_call(functools.partial(correction_kernel, SEQ_LEN, NSEQ), grid=...  16.9 us

profile of v3, /device:TPU:0, one launch (start us, length us, event | category | flops | bytes accessed | tf_op | source)
XLA Modules:
  0.0 187.3 jit_solution(3917218150805010855)
XLA Ops:
  0.0 170.4 %shard_map.55 = (bf16[512,896]{1,0:T(8,128)(2,1)}, bf16[16,2,256,256]{3,2,1,0:T(8,128)(2,1)}) custom-call(bf16[32,14336]{1,0:T(8,128)(2,1)} %x_ref.1, bf16[32,4096]{1,0:T(8,128)(2,1)} %g_ref.1, bf16[14336,896]{1,0:T(8,128)(2,1)} %ein_ref.1, bf16[256,4096]{1,0:T(8,128)(2,1)} %eout_ref.1), custom_call_target="tpu_custom_call" | custom-call | flops 14227079168 | bytes 25690112 | tf_op jit(solution)/shard_map/pallas_call | solution.py:252
  170.4 16.9 %shard_map.56 = f32[896,4096]{1,0:T(8,128)} custom-call(s32[4]{0:T(128)} %len_ref.1, bf16[512,896]{1,0:T(8,128)(2,1)} %get-tuple-element.7.pin_ref, bf16[16,512,256]{2,1,0:T(8,128)(2,1)} %bitcast.1), custom_call_target="tpu_custom_call" | custom-call | tf_op jit(solution)/shard_map/pallas_call | solution.py:312
